TPU v7x, 32 devices: a whole 2x2x4 slice. The times are simulated.
32 devices in a mesh: dp: 16 (over z, y, x), seq: 2 (over core).
Axes of the slice: x: 2, y: 2, z: 4, core: 2. Of those that a mesh axis runs over, the one named last changes fastest.
Arguments:
- tokens: bfloat16 [11200, 768], P(('dp', 'seq')), may hold values from -6 to 6
- crop_len: int32 [16, 10], P('dp'), may hold values from 19 to 197, as said below
- qkv_weight: bfloat16 [2, 768, 2304], replicated, may hold values from -0.3125 to 0.3125
- query_bias: float32 [2, 768], replicated, may hold values from -3 to 3
- value_bias: float32 [2, 768], replicated, may hold values from -3 to 3
- out_weight: bfloat16 [2, 768, 768], replicated, may hold values from -0.625 to 0.625
- out_bias: float32 [2, 768], replicated, may hold values from -3 to 3
- first_gain: float32 [2, 768], replicated, may hold values from 0.5 to 1.5
- first_shift: float32 [2, 768], replicated, may hold values from -3 to 3
- second_gain: float32 [2, 768], replicated, may hold values from 0.5 to 1.5
- second_shift: float32 [2, 768], replicated, may hold values from -3 to 3
- up_weight: bfloat16 [2, 768, 3072], replicated, may hold values from -0.21875 to 0.21875
- up_bias: float32 [2, 3072], replicated, may hold values from -3 to 3
- down_weight: bfloat16 [2, 3072, 768], replicated, may hold values from -0.109375 to 0.109375
- down_bias: float32 [2, 768], replicated, may hold values from -3 to 3
- cotangent: bfloat16 [11200, 768], P(('dp', 'seq')), may hold values from -6 to 6
Outputs:
- result: bfloat16 [11200, 768], P(('dp', 'seq'))
- grad_tokens: bfloat16 [11200, 768], P(('dp', 'seq'))
- grad_qkv_weight: float32 [2, 768, 2304], P(None, 'dp', 'seq')
- grad_query_bias: float32 [2, 768], P(None, 'dp')
- grad_value_bias: float32 [2, 768], P(None, 'dp')
- grad_out_weight: float32 [2, 768, 768], P(None, 'dp', 'seq')
- grad_out_bias: float32 [2, 768], P(None, 'dp')
- grad_first_gain: float32 [2, 768], P(None, 'dp')
- grad_first_shift: float32 [2, 768], P(None, 'dp')
- grad_second_gain: float32 [2, 768], P(None, 'dp')
- grad_second_shift: float32 [2, 768], P(None, 'dp')
- grad_up_weight: float32 [2, 768, 3072], P(None, 'dp', 'seq')
- grad_up_bias: float32 [2, 3072], P(None, 'dp')
- grad_down_weight: float32 [2, 3072, 768], P(None, 'dp', 'seq')
- grad_down_bias: float32 [2, 768], P(None, 'dp')
Inputs may be any that keep to these rules, and one draw needn't show every extreme that they name: `crop_len`: the first 2 entries of a row are global crops of 99 to 197 live tokens, the other 8 local crops of 19 to 37. The global crop that holds row 350 of its group has 197 live tokens.
All inputs are finite; a program needn't handle non-finite values.
Results may differ from a plain program's by a relative error of at most 0.019.
The roundings to bfloat16 on the way count: a program that leaves them out, or rounds other values in their place, can miss the bound.
Values may be sent and summed in bfloat16 or wider, within the bound.
No kernel may reach another device: no remote copies, remote signals or barrier semaphores. Data moves between devices by JAX's collectives and lax.ppermute only.
A program may use at most 256 MiB of HBM per device.

v0:
```python
from functools import partial

import jax
import jax.numpy as jnp
from jax import lax
from jax.sharding import PartitionSpec as P

HD = 64
GPAD = 198
LPAD = 38
IMG_DEV = 1


EPS = 1e-06
MASKED = -1e30
MATRIX_SLOTS = (0, 3, 9, 11)
VECTOR_SLOTS = (1, 2, 4, 5, 6, 7, 8, 10, 12)


def shortened(array):
    return jax.tree.map(lambda a: a.astype(jnp.bfloat16) if a.dtype == jnp.float32 else a, array)


def layer_norm(hidden, norm_gain, norm_shift):
    row_mean = jnp.mean(hidden, axis=-1, keepdims=True)
    centered = hidden - row_mean
    inverse = lax.rsqrt(jnp.mean(centered * centered, axis=-1, keepdims=True) + EPS)
    normed = centered * inverse
    return (normed * norm_gain + norm_shift, normed, inverse)


def norm_back(upstream, normed, inverse, norm_gain):
    scaled = upstream * norm_gain
    centered = scaled - jnp.mean(scaled, axis=-1, keepdims=True)
    centered = centered - normed * jnp.mean(scaled * normed, axis=-1, keepdims=True)
    return (centered * inverse, jnp.sum(upstream * normed, axis=0), jnp.sum(upstream, axis=0))


def crop_views(group_rows):
    split_at = 2 * IMG_DEV * GPAD
    wide_crops = group_rows[:split_at].reshape((2 * IMG_DEV, GPAD) + group_rows.shape[1:])
    narrow_crops = group_rows[split_at:].reshape((8 * IMG_DEV, LPAD) + group_rows.shape[1:])
    return (wide_crops, narrow_crops)


def join_views(wide_crops, narrow_crops):
    return jnp.concatenate(
        [
            wide_crops.reshape((-1,) + wide_crops.shape[2:]),
            narrow_crops.reshape((-1,) + narrow_crops.shape[2:]),
        ],
        axis=0,
    )


def crop_scores(queries, keys_in, lengths, scaling):
    scores = (
        jnp.einsum("cqhe,ckhe->chqk", queries, keys_in, preferred_element_type=jnp.float32)
        * scaling
    )
    positions = lax.broadcasted_iota(jnp.int32, scores.shape, 3)
    return jnp.where(positions < lengths[:, None, None, None], scores, MASKED)


def attend(queries, keys_in, values, lengths, scaling):
    scores = crop_scores(queries, keys_in, lengths, scaling)
    row_max = jnp.max(scores, axis=-1, keepdims=True)
    exponent = jnp.exp(scores - row_max)
    totals = jnp.sum(exponent, axis=-1, keepdims=True)
    weights = (exponent / totals).astype(jnp.bfloat16)
    mixed_rows = jnp.einsum("chqk,ckhe->cqhe", weights, values, preferred_element_type=jnp.float32)
    return (mixed_rows.astype(jnp.bfloat16), row_max + jnp.log(totals))


def attend_back(queries, keys_in, values, lengths, log_total, upstream, scaling):
    scores = crop_scores(queries, keys_in, lengths, scaling)
    weights = jnp.exp(scores - log_total)
    low_weights = weights.astype(jnp.bfloat16)
    grad_values = jnp.einsum(
        "chqk,cqhe->ckhe", low_weights, upstream, preferred_element_type=jnp.float32
    )
    grad_weights = jnp.einsum(
        "cqhe,ckhe->chqk", upstream, values, preferred_element_type=jnp.float32
    )
    row_dot = jnp.sum(weights * grad_weights, axis=-1, keepdims=True)
    grad_scores = (weights * (grad_weights - row_dot)).astype(jnp.bfloat16)
    grad_queries = (
        jnp.einsum("chqk,ckhe->cqhe", grad_scores, keys_in, preferred_element_type=jnp.float32)
        * scaling
    )
    grad_keys = (
        jnp.einsum("chqk,cqhe->ckhe", grad_scores, queries, preferred_element_type=jnp.float32)
        * scaling
    )
    return (grad_queries, grad_keys, grad_values)


def heads_attention(stacked, lengths):
    group_rows = stacked.shape[0]
    split_rows = stacked.reshape(group_rows, 3, -1, HD)
    wide_crops, narrow_crops = crop_views(split_rows)
    scaling = HD ** (-0.5)
    mixed_wide, log_wide = attend(
        wide_crops[:, :, 0],
        wide_crops[:, :, 1],
        wide_crops[:, :, 2],
        lengths[: 2 * IMG_DEV],
        scaling,
    )
    mixed_narrow, log_narrow = attend(
        narrow_crops[:, :, 0],
        narrow_crops[:, :, 1],
        narrow_crops[:, :, 2],
        lengths[2 * IMG_DEV :],
        scaling,
    )
    mixed_rows = join_views(mixed_wide, mixed_narrow)
    return (mixed_rows.reshape(group_rows, 1, -1), (log_wide, log_narrow))


def heads_attention_back(stacked, lengths, log_total, grad_heads):
    group_rows = stacked.shape[0]
    split_rows = stacked.reshape(group_rows, 3, -1, HD)
    upstream = grad_heads.reshape(group_rows, -1, HD)
    wide_crops, narrow_crops = crop_views(split_rows)
    up_wide, up_narrow = crop_views(upstream)
    scaling = HD ** (-0.5)
    wide_grads = attend_back(
        wide_crops[:, :, 0],
        wide_crops[:, :, 1],
        wide_crops[:, :, 2],
        lengths[: 2 * IMG_DEV],
        log_total[0],
        up_wide,
        scaling,
    )
    narrow_grads = attend_back(
        narrow_crops[:, :, 0],
        narrow_crops[:, :, 1],
        narrow_crops[:, :, 2],
        lengths[2 * IMG_DEV :],
        log_total[1],
        up_narrow,
        scaling,
    )
    wide_stack = jnp.stack(wide_grads, axis=2).astype(jnp.bfloat16)
    narrow_stack = jnp.stack(narrow_grads, axis=2).astype(jnp.bfloat16)
    return join_views(wide_stack, narrow_stack).reshape(group_rows, 3, 1, -1)


def layer_forward(hidden, weights, lengths):
    (
        qkv_w,
        query_b,
        value_b,
        out_w,
        out_b,
        gain_one,
        shift_one,
        gain_two,
        shift_two,
        up_w,
        up_b,
        down_w,
        down_b,
    ) = weights
    row_count, model_width = hidden.shape
    seq_parts = lax.axis_size("seq")
    normed_in, first_hat, first_inv = layer_norm(hidden, gain_one, shift_one)
    first_low = normed_in.astype(jnp.bfloat16)
    qkv_bias = jnp.concatenate([query_b, jnp.zeros_like(query_b), value_b])
    joint_rows = jnp.dot(first_low, qkv_w, preferred_element_type=jnp.float32) + qkv_bias
    joint_low = joint_rows.astype(jnp.bfloat16).reshape(
        row_count, 3, seq_parts, model_width // seq_parts
    )
    stacked = lax.all_to_all(joint_low, "seq", split_axis=2, concat_axis=0, tiled=True)
    mixed_rows, log_total = heads_attention(stacked, lengths)
    merged = lax.all_to_all(mixed_rows, "seq", split_axis=0, concat_axis=1, tiled=True).reshape(
        row_count, model_width
    )
    middle = hidden + jnp.dot(merged, out_w, preferred_element_type=jnp.float32) + out_b
    normed_mid, second_hat, second_inv = layer_norm(middle, gain_two, shift_two)
    second_low = normed_mid.astype(jnp.bfloat16)
    up_values = jnp.dot(second_low, up_w, preferred_element_type=jnp.float32) + up_b
    active = jax.nn.gelu(up_values, approximate=False).astype(jnp.bfloat16)
    output = middle + jnp.dot(active, down_w, preferred_element_type=jnp.float32) + down_b
    return (
        output,
        first_hat,
        first_inv,
        first_low,
        stacked,
        log_total,
        merged,
        second_hat,
        second_inv,
        second_low,
        up_values,
        active,
    )


def layer_backward(upstream, hidden, weights, lengths):
    (
        qkv_w,
        query_b,
        value_b,
        out_w,
        out_b,
        gain_one,
        shift_one,
        gain_two,
        shift_two,
        up_w,
        up_b,
        down_w,
        down_b,
    ) = weights
    saved_state = layer_forward(hidden, weights, lengths)
    (
        output,
        first_hat,
        first_inv,
        first_low,
        stacked,
        log_total,
        merged,
        second_hat,
        second_inv,
        second_low,
        up_values,
        active,
    ) = saved_state
    row_count, model_width = hidden.shape
    seq_parts = lax.axis_size("seq")
    grad_down = upstream.astype(jnp.bfloat16)
    down_w_grad = jnp.einsum("tf,td->fd", active, grad_down, preferred_element_type=jnp.float32)
    down_b_grad = jnp.sum(grad_down, axis=0, dtype=jnp.float32)
    grad_active = jnp.einsum("td,fd->tf", grad_down, down_w, preferred_element_type=jnp.float32)
    unused_value, gelu_pull = jax.vjp(partial(jax.nn.gelu, approximate=False), up_values)
    grad_up = gelu_pull(grad_active)[0].astype(jnp.bfloat16)
    up_w_grad = jnp.einsum("td,tf->df", second_low, grad_up, preferred_element_type=jnp.float32)
    up_b_grad = jnp.sum(grad_up, axis=0, dtype=jnp.float32)
    grad_normed = jnp.einsum("tf,df->td", grad_up, up_w, preferred_element_type=jnp.float32)
    grad_mid, gain_two_grad, shift_two_grad = norm_back(
        grad_normed, second_hat, second_inv, gain_two
    )
    grad_mid = grad_mid + upstream
    grad_branch = grad_mid.astype(jnp.bfloat16)
    out_w_grad = jnp.einsum("td,te->de", merged, grad_branch, preferred_element_type=jnp.float32)
    out_b_grad = jnp.sum(grad_branch, axis=0, dtype=jnp.float32)
    grad_merged = jnp.einsum(
        "te,de->td", grad_branch, out_w, preferred_element_type=jnp.float32
    ).astype(jnp.bfloat16)
    grad_heads = lax.all_to_all(
        grad_merged.reshape(row_count, seq_parts, model_width // seq_parts),
        "seq",
        split_axis=1,
        concat_axis=0,
        tiled=True,
    )
    grad_stacked = heads_attention_back(stacked, lengths, log_total, grad_heads)
    grad_joint = lax.all_to_all(
        grad_stacked, "seq", split_axis=0, concat_axis=2, tiled=True
    ).reshape(row_count, 3 * model_width)
    qkv_w_grad = jnp.einsum("td,tf->df", first_low, grad_joint, preferred_element_type=jnp.float32)
    joint_sums = jnp.sum(grad_joint, axis=0, dtype=jnp.float32)
    query_b_grad = joint_sums[:model_width]
    value_b_grad = joint_sums[2 * model_width :]
    grad_first = jnp.einsum("tf,df->td", grad_joint, qkv_w, preferred_element_type=jnp.float32)
    grad_in, gain_one_grad, shift_one_grad = norm_back(grad_first, first_hat, first_inv, gain_one)
    gradients = (
        qkv_w_grad,
        query_b_grad,
        value_b_grad,
        out_w_grad,
        out_b_grad,
        gain_one_grad,
        shift_one_grad,
        gain_two_grad,
        shift_two_grad,
        up_w_grad,
        up_b_grad,
        down_w_grad,
        down_b_grad,
    )
    return (grad_in + grad_mid, gradients)


def assemble(matrices, vectors):
    members = [None] * (len(MATRIX_SLOTS) + len(VECTOR_SLOTS))
    for place_at, slot_at in enumerate(MATRIX_SLOTS):
        members[slot_at] = matrices[place_at]
    for place_at, slot_at in enumerate(VECTOR_SLOTS):
        members[slot_at] = vectors[place_at]
    return tuple(members)


def reduce_stack(gradients):
    shares = lax.psum_scatter(gradients, "dp", scatter_dimension=1, tiled=True)
    matrices = jax.tree.map(
        lambda part: part.astype(jnp.float32),
        lax.psum_scatter(
            shortened(tuple((shares[slot_at] for slot_at in MATRIX_SLOTS))),
            "seq",
            scatter_dimension=2,
            tiled=True,
        ),
    )
    vectors = lax.psum(tuple((shares[slot_at] for slot_at in VECTOR_SLOTS)), "seq")
    return assemble(matrices, vectors)


def shards(
    tokens,
    crop_len,
    qkv_weight,
    query_bias,
    value_bias,
    out_weight,
    out_bias,
    first_gain,
    first_shift,
    second_gain,
    second_shift,
    up_weight,
    up_bias,
    down_weight,
    down_bias,
    cotangent,
):
    lengths = crop_len[0]
    stacks = (
        qkv_weight,
        query_bias,
        value_bias,
        out_weight,
        out_bias,
        first_gain,
        first_shift,
        second_gain,
        second_shift,
        up_weight,
        up_bias,
        down_weight,
        down_bias,
    )
    layer_count = qkv_weight.shape[0]
    member_count = len(stacks)
    inputs_kept = []
    attention_kept = []
    hidden = tokens.astype(jnp.float32)
    for layer_at in range(layer_count):
        weights = tuple((member[layer_at] for member in stacks))
        inputs_kept.append(hidden)
        saved_state = layer_forward(hidden, weights, lengths)
        attention_kept.append((saved_state[4], saved_state[5], saved_state[6]))
        hidden = saved_state[0]
    result = hidden.astype(jnp.bfloat16)
    upstream = cotangent.astype(jnp.float32)
    summed = [None] * layer_count
    for layer_at in reversed(range(layer_count)):
        weights = tuple((member[layer_at] for member in stacks))
        upstream, gradients = layer_backward(upstream, inputs_kept[layer_at], weights, lengths)
        summed[layer_at] = gradients
    stacked_grads = tuple(
        (
            jnp.stack([summed[layer_at][member_at] for layer_at in range(layer_count)])
            for member_at in range(member_count)
        )
    )
    outputs = reduce_stack(stacked_grads)
    grad_tokens = upstream.astype(jnp.bfloat16)
    return (
        result,
        grad_tokens,
        outputs[0],
        outputs[1],
        outputs[2],
        outputs[3],
        outputs[4],
        outputs[5],
        outputs[6],
        outputs[7],
        outputs[8],
        outputs[9],
        outputs[10],
        outputs[11],
        outputs[12],
    )


def solution(mesh):
    placed = (
        P(("dp", "seq"), None),
        P("dp", None),
        P(),
        P(),
        P(),
        P(),
        P(),
        P(),
        P(),
        P(),
        P(),
        P(),
        P(),
        P(),
        P(),
        P(("dp", "seq"), None),
    )
    return jax.shard_map(
        shards,
        mesh=mesh,
        in_specs=placed,
        out_specs=(
            P(("dp", "seq"), None),
            P(("dp", "seq"), None),
            P(None, "dp", "seq"),
            P(None, "dp"),
            P(None, "dp"),
            P(None, "dp", "seq"),
            P(None, "dp"),
            P(None, "dp"),
            P(None, "dp"),
            P(None, "dp"),
            P(None, "dp"),
            P(None, "dp", "seq"),
            P(None, "dp"),
            P(None, "dp", "seq"),
            P(None, "dp"),
        ),
        check_vma=False,
    )
```

profile of v0, /device:TPU:0, one launch (start us, length us, event | category | flops | bytes accessed | tf_op | source)
XLA Modules:
  0.0 2398.1 jit_solution(12414742885169252381)
XLA Ops:
  66.4 15.0 multiply_convert_fusion.1
  88.2 5.2 all_to_all.140
  128.9 6.5 all_to_all.141
  138.8 5.0 reduce.17
  150.4 15.4 multiply_convert_fusion
  165.8 6.1 convert_reduce_fusion
  235.1 5.0 reshape.520
  240.1 4.9 multiply_reduce_fusion.4
  246.1 8.7 convert_reduce_fusion.1
  323.1 5.5 all_to_all.143
  335.5 5.1 convolution_bitcast_fusion.5
  340.6 5.2 convolution_bitcast_fusion.4
  345.7 11.1 pad_maximum_fusion.2
  363.9 6.7 pad_maximum_fusion.1
  379.3 7.1 pad_maximum_fusion
  394.0 4.6 fusion.130
  405.7 224.9 %reduce-scatter.42.cloned.1.call-done = f32[2,48,2304]{2,1,0:T(8,128)} async-done(((f32[2,768,2304]{2,1,0:T(8,128)}), f32[2,48,2304]{2,1,0:T(8,128)}) %reduce-scatter.42.cloned.1.call-update) | async-done | bytes 884752 | tf_op jit(solution)/shard_map/reduce_scatter | solution.py:300
  635.0 286.1 %reduce-scatter.50.cloned.1.call-done = f32[2,192,768]{2,1,0:T(8,128)} async-done(((f32[2,3072,768]{2,1,0:T(8,128)}), f32[2,192,768]{2,1,0:T(8,128)}) %reduce-scatter.50.cloned.1.call-update) | async-done | bytes 1179664 | tf_op jit(solution)/shard_map/reduce_scatter | solution.py:300
  924.4 287.1 %reduce-scatter.46.cloned.1.call-done = f32[2,48,3072]{2,1,0:T(8,128)} async-done(((f32[2,768,3072]{2,1,0:T(8,128)}), f32[2,48,3072]{2,1,0:T(8,128)}) %reduce-scatter.46.cloned.1.call-update) | async-done | bytes 1179664 | tf_op jit(solution)/shard_map/reduce_scatter | solution.py:300
  1216.3 5.0 fusion.78
  1221.3 115.4 %reduce-scatter.74.cloned.1.call-done = f32[48,2]{1,0:T(8,128)} async-done(((f32[768,2]{1,0:T(8,128)}), f32[48,2]{1,0:T(8,128)}) %reduce-scatter.74.cloned.1.call-update) | async-done | bytes 400
  1337.5 125.1 %reduce-scatter.68.cloned.1.call-done = f32[48,2]{1,0:T(8,128)} async-done(((f32[768,2]{1,0:T(8,128)}), f32[48,2]{1,0:T(8,128)}) %reduce-scatter.68.cloned.1.call-update) | async-done | bytes 400
  1463.4 124.5 %reduce-scatter.60.cloned.1.call-done = f32[48,2]{1,0:T(8,128)} async-done(((f32[768,2]{1,0:T(8,128)}), f32[48,2]{1,0:T(8,128)}) %reduce-scatter.60.cloned.1.call-update) | async-done | bytes 400
  1588.7 125.2 %reduce-scatter.66.cloned.1.call-done = f32[48,2]{1,0:T(8,128)} async-done(((f32[768,2]{1,0:T(8,128)}), f32[48,2]{1,0:T(8,128)}) %reduce-scatter.66.cloned.1.call-update) | async-done | bytes 400
  1714.8 124.8 %reduce-scatter.54.cloned.1.call-done = f32[48,2]{1,0:T(8,128)} async-done(((f32[768,2]{1,0:T(8,128)}), f32[48,2]{1,0:T(8,128)}) %reduce-scatter.54.cloned.1.call-update) | async-done | bytes 400
  1840.4 125.1 %reduce-scatter.56.cloned.1.call-done = f32[48,2]{1,0:T(8,128)} async-done(((f32[768,2]{1,0:T(8,128)}), f32[48,2]{1,0:T(8,128)}) %reduce-scatter.56.cloned.1.call-update) | async-done | bytes 400
  1966.3 124.7 %reduce-scatter.64.cloned.1.call-done = f32[48,2]{1,0:T(8,128)} async-done(((f32[768,2]{1,0:T(8,128)}), f32[48,2]{1,0:T(8,128)}) %reduce-scatter.64.cloned.1.call-update) | async-done | bytes 400
  2091.7 125.1 %reduce-scatter.62.cloned.1.call-done = f32[48,2]{1,0:T(8,128)} async-done(((f32[768,2]{1,0:T(8,128)}), f32[48,2]{1,0:T(8,128)}) %reduce-scatter.62.cloned.1.call-update) | async-done | bytes 400
  2217.7 127.7 %reduce-scatter.70.cloned.1.call-done = f32[192,2]{1,0:T(8,128)} async-done(((f32[3072,2]{1,0:T(8,128)}), f32[192,2]{1,0:T(8,128)}) %reduce-scatter.70.cloned.1.call-update) | async-done | bytes 1552
  2355.9 10.1 reduce-scatter.52.cloned.1.call-done
  2368.6 8.8 reduce-scatter.72.cloned.1.call-done
  2380.2 9.0 reduce-scatter.48.cloned.1.call-done
  (613 shorter events, 315.5 us)
Async XLA Ops:
  19.7 6.4 all-to-all-start
  23.7 21.4 copy-start.136
  51.5 5.8 all-to-all-start.1
  65.2 19.2 slice-start.13
  66.3 18.1 slice-start.14
  147.9 24.1 %slice-start.1 = ((s8[9437184]{0:T(1024)(128)(4,1)}), s8[4194304]{0:T(1024)(128)(4,1)S(1)}, s32[]{:S(2)}) async-start(s8[9437184]{0:T(1024)(128)(4,1)} %bitcast.447), calls=%async_computation.43 | async-start | bytes 8388608
  150.0 24.6 %copy-start.4 = (f32[350,768]{1,0:T(8,128)}, f32[350,768]{1,0:T(8,128)S(1)}, u32[]{:S(2)}) copy-start(f32[350,768]{1,0:T(8,128)S(1)} %get-tuple-element.105) | copy-start | bytes 3225604
  150.1 24.6 %copy-start.88 = (f32[350]{0:T(512)}, f32[350]{0:T(512)S(1)}, u32[]{:S(2)}) copy-start(f32[350]{0:T(512)S(1)} %broadcast_multiply_fusion.8) | copy-start | bytes 4204
  150.3 24.3 %copy-start.104 = (f32[350]{0:T(512)}, f32[350]{0:T(512)S(1)}, u32[]{:S(2)}) copy-start(f32[350]{0:T(512)S(1)} %add_rsqrt_fusion) | copy-start | bytes 4204
  150.4 21.6 slice-start.2
  150.4 21.6 slice-start.3
  182.7 6.1 all-to-all-start.4
  224.5 7.3 all-to-all-start.5
  228.4 174.9 %reduce-scatter.44.cloned.1.call-start = ((), (), s32[]{:S(2)}) async-start(), calls=%async_computation.26 | async-start | bytes 5013504 | tf_op jit(solution)/shard_map/reduce_scatter | solution.py:300
  263.1 367.5 %reduce-scatter.42.cloned.1.call-start = ((), (), s32[]{:S(2)}) async-start(), calls=%async_computation.25 | async-start | bytes 15040512 | tf_op jit(solution)/shard_map/reduce_scatter | solution.py:300
  356.8 564.2 %reduce-scatter.50.cloned.1.call-start = ((), (), s32[]{:S(2)}) async-start(), calls=%async_computation.29 | async-start | bytes 20054016 | tf_op jit(solution)/shard_map/reduce_scatter | solution.py:300
  370.6 840.9 %reduce-scatter.46.cloned.1.call-start = ((), (), s32[]{:S(2)}) async-start(), calls=%async_computation.27 | async-start | bytes 20054016 | tf_op jit(solution)/shard_map/reduce_scatter | solution.py:300
  386.5 950.2 %reduce-scatter.74.cloned.1.call-start = ((), (), s32[]{:S(2)}) async-start(), calls=%async_computation.41 | async-start | bytes 417792
  388.1 1074.5 %reduce-scatter.68.cloned.1.call-start = ((), (), s32[]{:S(2)}) async-start(), calls=%async_computation.38 | async-start | bytes 417792
  389.3 1198.7 %reduce-scatter.60.cloned.1.call-start = ((), (), s32[]{:S(2)}) async-start(), calls=%async_computation.34 | async-start | bytes 417792
  390.4 1323.6 %reduce-scatter.66.cloned.1.call-start = ((), (), s32[]{:S(2)}) async-start(), calls=%async_computation.37 | async-start | bytes 417792
  391.7 1447.8 %reduce-scatter.54.cloned.1.call-start = ((), (), s32[]{:S(2)}) async-start(), calls=%async_computation.31 | async-start | bytes 417792
  392.8 1572.6 %reduce-scatter.56.cloned.1.call-start = ((), (), s32[]{:S(2)}) async-start(), calls=%async_computation.32 | async-start | bytes 417792
  393.9 1697.0 %reduce-scatter.64.cloned.1.call-start = ((), (), s32[]{:S(2)}) async-start(), calls=%async_computation.36 | async-start | bytes 417792
  399.6 1817.2 %reduce-scatter.62.cloned.1.call-start = ((), (), s32[]{:S(2)}) async-start(), calls=%async_computation.35 | async-start | bytes 417792
  400.7 1944.7 %reduce-scatter.70.cloned.1.call-start = ((), (), s32[]{:S(2)}) async-start(), calls=%async_computation.39 | async-start | bytes 1671168
  402.5 1951.5 %reduce-scatter.58.cloned.1.call-start = ((), (), s32[]{:S(2)}) async-start(), calls=%async_computation.33 | async-start | bytes 294912
  405.6 1960.3 %reduce-scatter.52.cloned.1.call-start = ((), (), s32[]{:S(2)}) async-start(), calls=%async_computation.30 | async-start | bytes 884736
  634.9 1742.5 %reduce-scatter.72.cloned.1.call-start = ((), (), s32[]{:S(2)}) async-start(), calls=%async_computation.40 | async-start | bytes 884736
  923.1 290.7 %copy-start.7 = (f32[350,768]{1,0:T(8,128)S(1)}, f32[350,768]{1,0:T(8,128)}, u32[]{:S(2)}) copy-start(f32[350,768]{1,0:T(8,128)} %copy-done.6) | copy-start | bytes 3225604
  924.3 292.0 %copy-start.126 = (f32[768]{0:T(1024)S(1)}, f32[768]{0:T(1024)}, u32[]{:S(2)}) copy-start(f32[768]{0:T(1024)} %get-tuple-element.31) | copy-start | bytes 9220
  924.3 1464.9 %reduce-scatter.48.cloned.1.call-start = ((), (), s32[]{:S(2)}) async-start(), calls=%async_computation.28 | async-start | bytes 884736 | tf_op jit(solution)/shard_map/reduce_scatter | solution.py:303
  (142 other events, 673.3 us)
Sparse Core Ops, SparseCore 0:
  263.2 140.0 reduce-scatter.43
  410.1 220.4 reduce-scatter.41
  636.4 284.6 reduce-scatter.49
  926.7 284.7 reduce-scatter.45
  1216.0 120.6 reduce-scatter.73
  1341.9 120.6 reduce-scatter.67
  1467.3 120.6 reduce-scatter.59
  1593.3 120.6 reduce-scatter.65
  1719.2 120.3 reduce-scatter.53
  1844.8 120.6 reduce-scatter.55
  1970.1 120.7 reduce-scatter.63
  2096.1 120.7 reduce-scatter.61
  2221.7 123.6 reduce-scatter.69
  2347.5 6.5 reduce-scatter.57
  2356.7 9.1 reduce-scatter.51
  2368.2 9.1 reduce-scatter.71
  2380.1 9.1 reduce-scatter.47
where the time goes:
time: 2410 us; the launch traced here: 2400 us
  waiting for transfers between devices  1950 us (81%)
  local copies, waits for them, and re-layouts  186 us (8%)
  matrix products  132 us (5%)
  other arithmetic  69.5 us (3%)
  blocking collectives  25.2 us (1%)
    unnamed x29, waiting for transfers between devices  1140 us
    reduce_scatter x4, waiting for transfers between devices, reduce_stack(): shares = lax.psum_scatter(gradients, 'dp', scatter_dimension=1, tiled=True)  799 us
    unnamed x356, local copies, waits for them, and re-layouts  64.3 us
  transfers between devices with their start and end apart: 21, of which 19 were waited for; matrix products, arithmetic and copies ran while one was open for 7% of the time, Pallas kernels for 0%

commit v1 on v0

--- a/solution.py
+++ b/solution.py
@@ -15,10 +15,6 @@
 MASKED = -1e30
 MATRIX_SLOTS = (0, 3, 9, 11)
 VECTOR_SLOTS = (1, 2, 4, 5, 6, 7, 8, 10, 12)
-
-
-def shortened(array):
-    return jax.tree.map(lambda a: a.astype(jnp.bfloat16) if a.dtype == jnp.float32 else a, array)
 
 
 def layer_norm(hidden, norm_gain, norm_shift):
@@ -296,18 +292,63 @@
     return tuple(members)
 
 
-def reduce_stack(gradients):
-    shares = lax.psum_scatter(gradients, "dp", scatter_dimension=1, tiled=True)
-    matrices = jax.tree.map(
-        lambda part: part.astype(jnp.float32),
-        lax.psum_scatter(
-            shortened(tuple((shares[slot_at] for slot_at in MATRIX_SLOTS))),
-            "seq",
-            scatter_dimension=2,
-            tiled=True,
-        ),
-    )
-    vectors = lax.psum(tuple((shares[slot_at] for slot_at in VECTOR_SLOTS)), "seq")
+def reduce_matrix(partial_sum, bit_order):
+    parts = lax.axis_size("dp")
+    core = lax.axis_index("seq")
+    place = lax.axis_index("dp")
+    rows, columns = partial_sum.shape
+    halves = partial_sum.reshape(rows, 2, columns // 2)
+    kept = lax.dynamic_index_in_dim(halves, core, 1, keepdims=False)
+    sent = lax.dynamic_index_in_dim(halves, 1 - core, 1, keepdims=False).astype(jnp.bfloat16)
+    total = kept + lax.ppermute(sent, "seq", [(0, 1), (1, 0)]).astype(jnp.float32)
+    bits = parts.bit_length() - 1
+    total = total.astype(jnp.bfloat16).reshape((2,) * bits + (rows // parts, columns // 2))
+    left = list(range(bits))
+    for bit in bit_order:
+        axis = left.index(bit)
+        left.remove(bit)
+        flip = 1 << (bits - 1 - bit)
+        mine = (place // flip) % 2
+        sent = lax.dynamic_index_in_dim(total, 1 - mine, axis, keepdims=False)
+        kept = lax.dynamic_index_in_dim(total, mine, axis, keepdims=False)
+        came = lax.ppermute(sent, "dp", [(i, i ^ flip) for i in range(parts)])
+        total = (kept.astype(jnp.float32) + came.astype(jnp.float32)).astype(jnp.bfloat16)
+    return total.reshape(rows // parts, columns // 2).astype(jnp.float32)
+
+
+def reduce_vector(partial_sum):
+    parts = lax.axis_size("dp")
+    place = lax.axis_index("dp")
+    total = partial_sum + lax.ppermute(partial_sum, "seq", [(0, 1), (1, 0)])
+    bits = parts.bit_length() - 1
+    total = total.reshape((2,) * bits + (-1,))
+    for bit in range(bits):
+        flip = 1 << (bits - 1 - bit)
+        mine = (place // flip) % 2
+        sent = lax.dynamic_index_in_dim(total, 1 - mine, 0, keepdims=False)
+        kept = lax.dynamic_index_in_dim(total, mine, 0, keepdims=False)
+        total = kept + lax.ppermute(sent, "dp", [(i, i ^ flip) for i in range(parts)])
+    return total
+
+
+def reduce_layer(gradients, layer_at):
+    bits = lax.axis_size("dp").bit_length() - 1
+    order = list(range(bits))[::-1]
+    matrices = []
+    for place_at, slot_at in enumerate(MATRIX_SLOTS):
+        turn = (place_at + layer_at) % bits
+        matrices.append(reduce_matrix(gradients[slot_at], order[turn:] + order[:turn]))
+    parts = lax.axis_size("dp")
+    sizes = [gradients[slot_at].shape[0] // parts for slot_at in VECTOR_SLOTS]
+    packed = jnp.concatenate(
+        [gradients[slot_at].reshape(parts, -1) for slot_at in VECTOR_SLOTS], axis=1
+    )
+    total = reduce_vector(packed)
+    vectors = []
+    begin = 0
+    for size in sizes:
+        vectors.append(total[begin : begin + size])
+        begin += size
     return assemble(matrices, vectors)
 
 
@@ -362,14 +403,13 @@
     for layer_at in reversed(range(layer_count)):
         weights = tuple((member[layer_at] for member in stacks))
         upstream, gradients = layer_backward(upstream, inputs_kept[layer_at], weights, lengths)
-        summed[layer_at] = gradients
-    stacked_grads = tuple(
+        summed[layer_at] = reduce_layer(gradients, layer_at)
+    outputs = tuple(
         (
             jnp.stack([summed[layer_at][member_at] for layer_at in range(layer_count)])
             for member_at in range(member_count)
         )
     )
-    outputs = reduce_stack(stacked_grads)
     grad_tokens = upstream.astype(jnp.bfloat16)
     return (
         result,

time: 2410 us -> 764 us (0.32)
  waiting for transfers between devices: 1950 us -> 198 us
  local copies, waits for them, and re-layouts: 186 us -> 264 us
  starting transfers between devices: 17.1 us -> 91.7 us
    unnamed x29 -> x0, waiting for transfers between devices: 1140 us -> none
    reduce_scatter x5 -> x0, waiting for transfers between devices: 808 us -> none  [the longest x4 799 us: reduce_stack(): shares = lax.psum_scatter(gradients, 'dp', scatter_dimension=1, tiled=True)]
    ppermute x0 -> x50, waiting for transfers between devices: none -> 190 us  [the longest x32 177 us: reduce_matrix(): came = lax.ppermute(sent, 'dp', [(i, i ^ flip) for i in range(parts)])]
    ppermute x0 -> x50, starting transfers between devices: none -> 67.9 us  [the longest x32 46.9 us: reduce_matrix(): came = lax.ppermute(sent, 'dp', [(i, i ^ flip) for i in range(parts)])]
    dynamic_slice x0 -> x24, local copies, waits for them, and re-layouts: none -> 50.2 us  [the longest x6 30.8 us: reduce_matrix(): kept = lax.dynamic_index_in_dim(halves, core, 1, keepdims=False)]
    reshape x0 -> x20, local copies, waits for them, and re-layouts: none -> 32.3 us  [the longest x2 26.5 us: reduce_matrix(): halves = partial_sum.reshape(rows, 2, columns // 2)]
    unnamed x356 -> x370, local copies, waits for them, and re-layouts: 64.3 us -> 51.3 us
  transfers between devices with their start and end apart: 21 -> 56, of which waited for: 19 -> 33; matrix products, arithmetic and copies ran while one was open for 7% -> 38% of each run, Pallas kernels for 0% -> 0%
where the time goes in v1:
time: 764 us; the launch traced here: 757 us
  local copies, waits for them, and re-layouts  264 us (35%)
  waiting for transfers between devices  198 us (26%)
  matrix products  128 us (17%)
  starting transfers between devices  91.7 us (12%)
  other arithmetic  60.1 us (8%)
  blocking collectives  11.5 us (2%)
    ppermute x32, waiting for transfers between devices, reduce_matrix(): came = lax.ppermute(sent, 'dp', [(i, i ^ flip) for i in range(parts)])  177 us
    unnamed x370, local copies, waits for them, and re-layouts  51.3 us
    ppermute x32, starting transfers between devices, reduce_matrix(): came = lax.ppermute(sent, 'dp', [(i, i ^ flip) for i in range(parts)])  46.9 us
    dynamic_slice x6, local copies, waits for them, and re-layouts, reduce_matrix(): kept = lax.dynamic_index_in_dim(halves, core, 1, keepdims=False)  30.8 us
    dot_general x2, matrix products, layer_forward(): jnp.dot(second_low, up_w, preferred_element_type=jnp.float32) + up_b  30.3 us
    reshape x2, local copies, waits for them, and re-layouts, reduce_matrix(): halves = partial_sum.reshape(rows, 2, columns // 2)  26.5 us
    ppermute x8, starting transfers between devices, reduce_vector(): lax.ppermute(sent, 'dp', [(i, i ^ flip) for i in range(parts)])  18.1 us
    dynamic_slice x4, local copies, waits for them, and re-layouts, reduce_matrix(): lax.dynamic_index_in_dim(halves, 1 - core, 1, keepdims=False)  18.1 us
  transfers between devices with their start and end apart: 56, of which 33 were waited for; matrix products, arithmetic and copies ran while one was open for 38% of the time, Pallas kernels for 0%

profile of v1, /device:TPU:0, one launch (start us, length us, event | category | flops | bytes accessed | tf_op | source)
XLA Modules:
  0.0 757.1 jit_solution(11455439805319601634)
XLA Ops:
  59.9 15.1 %multiply_convert_fusion.1 = (bf16[350,3072]{1,0:T(8,128)(2,1)S(1)}, f32[350,3072]{1,0:T(8,128)}, f32[350,3072]{1,0:T(8,128)}) fusion(f32[3072]{0:T(1024)S(1)} %bitcast.748, bf16[2,768,3072]{2,1,0:T(8,128)(2,1)} %param.27, f32[350,768]{1,0:T(8,128)S(1)} %get-tuple-element.122, f32[768]{0:T(1024)S(1)} %get-tuple-element.36, f32[768]{0:T(1024)S(1)} %get-tuple-element.153, ...), kind=kOutput, calls=%fused_computation.49 | convolution fusion | flops 1723814400 | bytes 16567024 | tf_op jit(solution)/shard_map/dot_general | solution.py:180
  81.8 5.2 all_to_all.140
  120.9 6.3 all_to_all.141
  130.5 5.0 reduce.17
  142.1 15.2 %multiply_convert_fusion = (bf16[350,3072]{1,0:T(8,128)(2,1)}, f32[350,3072]{1,0:T(8,128)}, f32[350,3072]{1,0:T(8,128)}) fusion(f32[3072]{0:T(1024)S(1)} %bitcast.747, bf16[2,768,3072]{2,1,0:T(8,128)(2,1)} %param.27, f32[350,768]{1,0:T(8,128)S(1)} %get-tuple-element.131, f32[768]{0:T(1024)S(1)} %get-tuple-element.35, f32[768]{0:T(1024)S(1)} %get-tuple-element.154, ...), kind=kOutput, calls=%fused_computation.36 | convolution fusion | flops 1723814400 | bytes 16567024 | tf_op jit(solution)/shard_map/dot_general | solution.py:180
  157.4 6.5 convert_reduce_fusion
  242.4 5.2 multiply_reduce_fusion.3
  251.1 8.2 %convert_reduce_fusion.1 = (f32[3072]{0:T(1024)}, bf16[350,3072]{1,0:T(8,128)(2,1)S(1)}) fusion(f32[350,3072]{1,0:T(8,128)} %get-tuple-element.64, f32[350,3072]{1,0:T(8,128)} %get-tuple-element.123, bf16[2,3072,768]{2,1,0:T(8,128)(2,1)} %param.29, f32[350,768]{1,0:T(8,128)S(1)} %get-tuple-element.56), kind=kOutput, calls=%fused_computation.33 | convolution fusion | flops 1668976128 | bytes 16607232 | tf_op jit(solution)/shard_map/td,fd->tf/dot_general | solution.py:235
  259.3 5.9 multiply_reduce_fusion.4
  347.9 7.1 fusion.263
  355.1 5.5 fusion.264
  360.5 13.3 %reshape.722 = f32[768,2,1536]{2,1,0:T(2,128)} reshape(f32[768,3072]{1,0:T(8,128)} %fusion.263) | data formatting | bytes 18874368 | tf_op jit(solution)/shard_map/reshape | solution.py:300
  373.8 7.6 %constant_dynamic-slice_fusion.10 = bf16[768,1,1536]{2,1,0:T(2,128)(2,1)} fusion(f32[768,2,1536]{2,1,0:T(2,128)} %reshape.722, s32[]{:T(128)S(6)} %select_n.314), kind=kLoop, calls=%fused_computation.422 | loop fusion | bytes 4718596 | tf_op jit(solution)/shard_map/jit(dynamic_index_in_dim)/dynamic_slice | solution.py:302
  381.5 7.7 %constant_dynamic-slice_fusion.11 = f32[768,1,1536]{2,1,0:T(1,128)} fusion(f32[768,2,1536]{2,1,0:T(2,128)} %reshape.722, s32[]{:T(128)S(6)} %select_n.313), kind=kLoop, calls=%fused_computation.423 | loop fusion | bytes 9437188 | tf_op jit(solution)/shard_map/jit(dynamic_index_in_dim)/dynamic_slice | solution.py:301
  389.1 13.1 %reshape.724 = f32[768,2,1536]{2,1,0:T(2,128)} reshape(f32[768,3072]{1,0:T(8,128)} %fusion.264) | data formatting | bytes 18874368 | tf_op jit(solution)/shard_map/reshape | solution.py:300
  402.3 8.4 %constant_dynamic-slice_fusion.8 = bf16[768,1,1536]{2,1,0:T(2,128)(2,1)} fusion(f32[768,2,1536]{2,1,0:T(2,128)} %reshape.724, s32[]{:T(128)S(6)} %select_n.314), kind=kLoop, calls=%fused_computation.420 | loop fusion | bytes 4718596 | tf_op jit(solution)/shard_map/jit(dynamic_index_in_dim)/dynamic_slice | solution.py:302
  410.7 5.1 constant_dynamic-slice_fusion.9
  432.5 4.7 dot_general.219
  453.9 6.1 copy.341
  462.5 6.2 copy.343
  515.6 5.9 collective-permute-done.26
  523.3 6.5 collective-permute-done.21
  532.4 5.5 collective-permute-done.27
  538.5 4.6 collective-permute-done.22
  578.0 8.7 %collective-permute-done.6 = bf16[2,2,2,48,1152]{4,3,2,0,1:T(8,128)(2,1)} collective-permute-done((bf16[2,2,2,48,1152]{4,3,2,0,1:T(8,128)(2,1)S(1)}, bf16[2,2,2,48,1152]{4,3,2,0,1:T(8,128)(2,1)}, u32[]{:S(2)}, u32[]{:S(2)}) %collective-permute-start.6) | collective-permute-done | bytes 884768 | tf_op jit(solution)/shard_map/ppermute | solution.py:314
  593.1 63.3 %collective-permute-done.7 = bf16[2,2,48,1152]{3,2,1,0:T(8,128)(2,1)S(1)} collective-permute-done((bf16[2,2,48,1152]{3,2,1,0:T(8,128)(2,1)S(1)}, bf16[2,2,48,1152]{3,2,1,0:T(8,128)(2,1)S(1)}, u32[]{:S(2)}, u32[]{:S(2)}) %collective-permute-start.7) | collective-permute-done | bytes 442400 | tf_op jit(solution)/shard_map/ppermute | solution.py:314
  657.2 9.7 %collective-permute-done.2 = bf16[2,2,48,1152]{3,2,0,1:T(8,128)(2,1)S(1)} collective-permute-done((bf16[2,2,48,1152]{3,2,0,1:T(8,128)(2,1)S(1)}, bf16[2,2,48,1152]{3,2,0,1:T(8,128)(2,1)S(1)}, u32[]{:S(2)}, u32[]{:S(2)}) %collective-permute-start.2) | collective-permute-done | bytes 442400 | tf_op jit(solution)/shard_map/ppermute | solution.py:314
  671.2 15.3 %collective-permute-done.8 = bf16[2,48,1152]{2,1,0:T(8,128)(2,1)S(1)} collective-permute-done((bf16[2,48,1152]{2,1,0:T(8,128)(2,1)S(1)}, bf16[2,48,1152]{2,1,0:T(8,128)(2,1)S(1)}, u32[]{:S(2)}, u32[]{:S(2)}) %collective-permute-start.8) | collective-permute-done | bytes 221216 | tf_op jit(solution)/shard_map/ppermute | solution.py:314
  686.6 5.8 collective-permute-done.3
  698.4 5.3 collective-permute-done.4
  709.2 19.9 %collective-permute-done.32 = bf16[2,2,48,1536]{3,2,1,0:T(8,128)(2,1)S(1)} collective-permute-done((bf16[2,2,48,1536]{3,2,1,0:T(8,128)(2,1)S(1)}, bf16[2,2,48,1536]{3,2,1,0:T(8,128)(2,1)S(1)}, u32[]{:S(2)}, u32[]{:S(2)}) %collective-permute-start.32) | collective-permute-done | bytes 589856 | tf_op jit(solution)/shard_map/ppermute | solution.py:314
  733.8 8.3 %collective-permute-start.48 = (bf16[2,192,384]{2,1,0:T(8,128)(2,1)S(1)}, bf16[2,192,384]{2,1,0:T(8,128)(2,1)S(1)}, u32[]{:S(2)}, u32[]{:S(2)}) collective-permute-start(bf16[2,192,384]{2,1,0:T(8,128)(2,1)S(1)} %dynamic-slice_bitcast_fusion.8), channel_id=1, source_target_pairs={{0,8},{2,10},{4,12},{6,14},{8,0},{10,2},{12,4},{14,6},{16,24},{18,... | collective-permute-start | bytes 884744 | tf_op jit(solution)/shard_map/ppermute | solution.py:314
  (811 shorter events, 437.0 us)
Async XLA Ops:
  174.8 16.7 %all-to-all-start.4 = ((bf16[350,2,384]{2,0,1:T(8,128)(2,1)}), bf16[350,2,384]{2,0,1:T(8,128)(2,1)}, u32[]{:S(2)}, u32[]{:S(2)}) async-start(bf16[350,2,384]{2,0,1:T(8,128)(2,1)} %copy.279), calls=%async_computation.4 | async-start | bytes 1081344 | tf_op jit(solution)/shard_map/all_to_all | solution.py:251
  191.0 319.0 %collective-permute-start.25 = (bf16[768,384]{1,0:T(8,128)(2,1)}, bf16[768,384]{1,0:T(8,128)(2,1)}, u32[]{:S(2)}, u32[]{:S(2)}) collective-permute-start(bf16[768,384]{1,0:T(8,128)(2,1)} %fusion.169), channel_id=1, source_target_pairs={{0,1},{1,0},{2,3},{3,2},{4,5},{5,4},{6,7},{7,6},{8,9},{9,8},{10,11... | collective-permute-start | bytes 1769480 | tf_op jit(solution)/shard_map/ppermute | solution.py:303
  250.9 220.3 %collective-permute-start.15 = (f32[16,576]{1,0:T(8,128)}, f32[16,576]{1,0:T(8,128)}, u32[]{:S(2)}, u32[]{:S(2)}) collective-permute-start(f32[16,576]{1,0:T(8,128)} %concatenate.87), channel_id=1, source_target_pairs={{0,1},{1,0},{2,3},{3,2},{4,5},{5,4},{6,7},{7,6},{8,9},{9,8},{10,11... | collective-permute-start | bytes 110600 | tf_op jit(solution)/shard_map/ppermute | solution.py:322
  269.6 11.1 %all-to-all-start.6 = ((bf16[350,2,384]{2,0,1:T(8,128)(2,1)}), bf16[350,2,384]{2,0,1:T(8,128)(2,1)S(1)}, u32[]{:S(2)}, u32[]{:S(2)}) async-start(bf16[350,2,384]{2,0,1:T(8,128)(2,1)} %copy.302), calls=%async_computation.6 | async-start | bytes 1081344 | tf_op jit(solution)/shard_map/all_to_all | solution.py:251
  280.1 232.2 %collective-permute-start.20 = (bf16[768,384]{1,0:T(8,128)(2,1)}, bf16[768,384]{1,0:T(8,128)(2,1)}, u32[]{:S(2)}, u32[]{:S(2)}) collective-permute-start(bf16[768,384]{1,0:T(8,128)(2,1)} %fusion.168), channel_id=1, source_target_pairs={{0,1},{1,0},{2,3},{3,2},{4,5},{5,4},{6,7},{7,6},{8,9},{9,8},{10,11... | collective-permute-start | bytes 1769480 | tf_op jit(solution)/shard_map/ppermute | solution.py:303
  337.3 134.9 %collective-permute-start.10 = (f32[16,576]{1,0:T(8,128)}, f32[16,576]{1,0:T(8,128)}, u32[]{:S(2)}, u32[]{:S(2)}) collective-permute-start(f32[16,576]{1,0:T(8,128)} %concatenate.86), channel_id=1, source_target_pairs={{0,1},{1,0},{2,3},{3,2},{4,5},{5,4},{6,7},{7,6},{8,9},{9,8},{10,11... | collective-permute-start | bytes 110600 | tf_op jit(solution)/shard_map/ppermute | solution.py:322
  347.5 214.6 %collective-permute-start.5 = (bf16[768,1152]{1,0:T(8,128)(2,1)}, bf16[768,1152]{1,0:T(8,128)(2,1)}, u32[]{:S(2)}, u32[]{:S(2)}) collective-permute-start(bf16[768,1152]{1,0:T(8,128)(2,1)} %fusion.75), channel_id=1, source_target_pairs={{0,1},{1,0},{2,3},{3,2},{4,5},{5,4},{6,7},{7,6},{8,9},{9,8},{10,11... | collective-permute-start | bytes 5308424 | tf_op jit(solution)/shard_map/ppermute | solution.py:303
  471.2 93.8 %collective-permute-start = (bf16[768,1152]{1,0:T(8,128)(2,1)}, bf16[768,1152]{1,0:T(8,128)(2,1)}, u32[]{:S(2)}, u32[]{:S(2)}) collective-permute-start(bf16[768,1152]{1,0:T(8,128)(2,1)} %fusion.74), channel_id=1, source_target_pairs={{0,1},{1,0},{2,3},{3,2},{4,5},{5,4},{6,7},{7,6},{8,9},{9,8},{10,11... | collective-permute-start | bytes 5308424 | tf_op jit(solution)/shard_map/ppermute | solution.py:303
  504.6 63.9 %collective-permute-start.30 = (bf16[768,1536]{1,0:T(8,128)(2,1)}, bf16[768,1536]{1,0:T(8,128)(2,1)S(1)}, u32[]{:S(2)}, u32[]{:S(2)}) collective-permute-start(bf16[768,1536]{1,0:T(8,128)(2,1)} %bitcast.729), channel_id=1, source_target_pairs={{0,1},{1,0},{2,3},{3,2},{4,5},{5,4},{6,7},{7,6},{8,9},{9,8},{10,11... | collective-permute-start | bytes 7077896 | tf_op jit(solution)/shard_map/ppermute | solution.py:303
  510.0 61.1 %collective-permute-start.35 = (bf16[768,1536]{1,0:T(8,128)(2,1)}, bf16[768,1536]{1,0:T(8,128)(2,1)S(1)}, u32[]{:S(2)}, u32[]{:S(2)}) collective-permute-start(bf16[768,1536]{1,0:T(8,128)(2,1)} %bitcast.728), channel_id=1, source_target_pairs={{0,1},{1,0},{2,3},{3,2},{4,5},{5,4},{6,7},{7,6},{8,9},{9,8},{10,11... | collective-permute-start | bytes 7077896 | tf_op jit(solution)/shard_map/ppermute | solution.py:303
  512.3 9.1 %collective-permute-start.26 = (bf16[2,2,2,48,384]{4,3,1,2,0:T(8,128)(2,1)S(1)}, bf16[2,2,2,48,384]{4,3,1,2,0:T(8,128)(2,1)S(1)}, u32[]{:S(2)}, u32[]{:S(2)}) collective-permute-start(bf16[2,2,2,48,384]{4,3,1,2,0:T(8,128)(2,1)S(1)} %bitcast.745), channel_id=1, source_target_pairs={{0,8},{2,10},{4,12},{6,14},{8,0},{10,2},{12,4},{14,6},{16,24},{18,... | collective-permute-start | bytes 884744 | tf_op jit(solution)/shard_map/ppermute | solution.py:314
  521.5 8.2 %collective-permute-start.21 = (bf16[2,2,2,48,384]{4,3,2,0,1:T(8,128)(2,1)S(1)}, bf16[2,2,2,48,384]{4,3,2,0,1:T(8,128)(2,1)S(1)}, u32[]{:S(2)}, u32[]{:S(2)}) collective-permute-start(bf16[2,2,2,48,384]{4,3,2,0,1:T(8,128)(2,1)S(1)} %bitcast.746), channel_id=1, source_target_pairs={{0,4},{2,6},{4,0},{6,2},{8,12},{10,14},{12,8},{14,10},{16,20},{18,... | collective-permute-start | bytes 884744 | tf_op jit(solution)/shard_map/ppermute | solution.py:314
  561.4 11.4 %collective-permute-start.40 = (bf16[3072,384]{1,0:T(8,128)(2,1)}, bf16[3072,384]{1,0:T(8,128)(2,1)S(1)}, u32[]{:S(2)}, u32[]{:S(2)}) collective-permute-start(bf16[3072,384]{1,0:T(8,128)(2,1)} %bitcast.733), channel_id=1, source_target_pairs={{0,1},{1,0},{2,3},{3,2},{4,5},{5,4},{6,7},{7,6},{8,9},{9,8},{10,11... | collective-permute-start | bytes 7077896 | tf_op jit(solution)/shard_map/ppermute | solution.py:303
  562.1 14.7 %collective-permute-start.45 = (bf16[3072,384]{1,0:T(8,128)(2,1)S(1)}, bf16[3072,384]{1,0:T(8,128)(2,1)S(1)}, u32[]{:S(2)}, u32[]{:S(2)}) collective-permute-start(bf16[3072,384]{1,0:T(8,128)(2,1)S(1)} %bitcast.732), channel_id=1, source_target_pairs={{0,1},{1,0},{2,3},{3,2},{4,5},{5,4},{6,7},{7,6},{8,9},{9,8},{10,11... | collective-permute-start | bytes 7077896 | tf_op jit(solution)/shard_map/ppermute | solution.py:303
  565.0 21.6 %collective-permute-start.6 = (bf16[2,2,2,48,1152]{4,3,2,0,1:T(8,128)(2,1)S(1)}, bf16[2,2,2,48,1152]{4,3,2,0,1:T(8,128)(2,1)}, u32[]{:S(2)}, u32[]{:S(2)}) collective-permute-start(bf16[2,2,2,48,1152]{4,3,2,0,1:T(8,128)(2,1)S(1)} %bitcast.742), channel_id=1, source_target_pairs={{0,4},{2,6},{4,0},{6,2},{8,12},{10,14},{12,8},{14,10},{16,20},{18,... | collective-permute-start | bytes 2654216 | tf_op jit(solution)/shard_map/ppermute | solution.py:314
  568.5 22.7 %collective-permute-start.1 = (bf16[2,2,2,48,1152]{4,3,0,1,2:T(8,128)(2,1)S(1)}, bf16[2,2,2,48,1152]{4,3,0,1,2:T(8,128)(2,1)}, u32[]{:S(2)}, u32[]{:S(2)}) collective-permute-start(bf16[2,2,2,48,1152]{4,3,0,1,2:T(8,128)(2,1)S(1)} %bitcast.743), channel_id=1, source_target_pairs={{0,2},{2,0},{4,6},{6,4},{8,10},{10,8},{12,14},{14,12},{16,18},{18,... | collective-permute-start | bytes 2654216 | tf_op jit(solution)/shard_map/ppermute | solution.py:314
  571.1 133.4 %collective-permute-start.31 = (bf16[2,2,2,48,1536]{4,3,2,1,0:T(8,128)(2,1)S(1)}, bf16[2,2,2,48,1536]{4,3,2,1,0:T(8,128)(2,1)S(1)}, u32[]{:S(2)}, u32[]{:S(2)}) collective-permute-start(bf16[2,2,2,48,1536]{4,3,2,1,0:T(8,128)(2,1)S(1)} %dynamic-slice_bitcast_fusion.1), channel_id=1, source_target_pairs={{0,8},{2,10},{4,12},{6,14},{8,0},{10,2},{12,4},{14,6},{16,24},{18,... | collective-permute-start | bytes 3538952 | tf_op jit(solution)/shard_map/ppermute | solution.py:314
  572.9 132.5 %collective-permute-start.36 = (bf16[2,2,2,48,1536]{4,3,0,1,2:T(8,128)(2,1)S(1)}, bf16[2,2,2,48,1536]{4,3,0,1,2:T(8,128)(2,1)S(1)}, u32[]{:S(2)}, u32[]{:S(2)}) collective-permute-start(bf16[2,2,2,48,1536]{4,3,0,1,2:T(8,128)(2,1)S(1)} %bitcast.740), channel_id=1, source_target_pairs={{0,16},{2,18},{4,20},{6,22},{8,24},{10,26},{12,28},{14,30},{16,0},... | collective-permute-start | bytes 3538952 | tf_op jit(solution)/shard_map/ppermute | solution.py:314
  576.8 130.6 %collective-permute-start.41 = (bf16[2,2,2,192,384]{4,3,2,1,0:T(8,128)(2,1)S(1)}, bf16[2,2,2,192,384]{4,3,2,1,0:T(8,128)(2,1)S(1)}, u32[]{:S(2)}, u32[]{:S(2)}) collective-permute-start(bf16[2,2,2,192,384]{4,3,2,1,0:T(8,128)(2,1)S(1)} %dynamic-slice_bitcast_fusion), channel_id=1, source_target_pairs={{0,16},{2,18},{4,20},{6,22},{8,24},{10,26},{12,28},{14,30},{16,0},... | collective-permute-start | bytes 3538952 | tf_op jit(solution)/shard_map/ppermute | solution.py:314
  586.7 121.6 %collective-permute-start.46 = (bf16[2,2,2,192,384]{4,3,0,1,2:T(8,128)(2,1)S(1)}, bf16[2,2,2,192,384]{4,3,0,1,2:T(8,128)(2,1)S(1)}, u32[]{:S(2)}, u32[]{:S(2)}) collective-permute-start(bf16[2,2,2,192,384]{4,3,0,1,2:T(8,128)(2,1)S(1)} %bitcast.741), channel_id=1, source_target_pairs={{0,2},{2,0},{4,6},{6,4},{8,10},{10,8},{12,14},{14,12},{16,18},{18,... | collective-permute-start | bytes 3538952 | tf_op jit(solution)/shard_map/ppermute | solution.py:314
  591.2 65.2 %collective-permute-start.7 = (bf16[2,2,48,1152]{3,2,1,0:T(8,128)(2,1)S(1)}, bf16[2,2,48,1152]{3,2,1,0:T(8,128)(2,1)S(1)}, u32[]{:S(2)}, u32[]{:S(2)}) collective-permute-start(bf16[2,2,48,1152]{3,2,1,0:T(8,128)(2,1)S(1)} %dynamic-slice_bitcast_fusion.6), channel_id=1, source_target_pairs={{0,8},{2,10},{4,12},{6,14},{8,0},{10,2},{12,4},{14,6},{16,24},{18,... | collective-permute-start | bytes 1327112 | tf_op jit(solution)/shard_map/ppermute | solution.py:314
  656.4 10.5 %collective-permute-start.2 = (bf16[2,2,48,1152]{3,2,0,1:T(8,128)(2,1)S(1)}, bf16[2,2,48,1152]{3,2,0,1:T(8,128)(2,1)S(1)}, u32[]{:S(2)}, u32[]{:S(2)}) collective-permute-start(bf16[2,2,48,1152]{3,2,0,1:T(8,128)(2,1)S(1)} %dynamic-slice_bitcast_fusion.7), channel_id=1, source_target_pairs={{0,4},{2,6},{4,0},{6,2},{8,12},{10,14},{12,8},{14,10},{16,20},{18,... | collective-permute-start | bytes 1327112 | tf_op jit(solution)/shard_map/ppermute | solution.py:314
  666.9 19.6 %collective-permute-start.8 = (bf16[2,48,1152]{2,1,0:T(8,128)(2,1)S(1)}, bf16[2,48,1152]{2,1,0:T(8,128)(2,1)S(1)}, u32[]{:S(2)}, u32[]{:S(2)}) collective-permute-start(bf16[2,48,1152]{2,1,0:T(8,128)(2,1)S(1)} %dynamic-slice_bitcast_fusion.12), channel_id=1, source_target_pairs={{0,16},{2,18},{4,20},{6,22},{8,24},{10,26},{12,28},{14,30},{16,0},... | collective-permute-start | bytes 663560 | tf_op jit(solution)/shard_map/ppermute | solution.py:314
  704.9 24.3 %collective-permute-start.32 = (bf16[2,2,48,1536]{3,2,1,0:T(8,128)(2,1)S(1)}, bf16[2,2,48,1536]{3,2,1,0:T(8,128)(2,1)S(1)}, u32[]{:S(2)}, u32[]{:S(2)}) collective-permute-start(bf16[2,2,48,1536]{3,2,1,0:T(8,128)(2,1)S(1)} %dynamic-slice_bitcast_fusion.5), channel_id=1, source_target_pairs={{0,16},{2,18},{4,20},{6,22},{8,24},{10,26},{12,28},{14,30},{16,0},... | collective-permute-start | bytes 1769480 | tf_op jit(solution)/shard_map/ppermute | solution.py:314
  705.7 25.3 %collective-permute-start.37 = (bf16[2,2,48,1536]{3,2,0,1:T(8,128)(2,1)S(1)}, bf16[2,2,48,1536]{3,2,0,1:T(8,128)(2,1)S(1)}, u32[]{:S(2)}, u32[]{:S(2)}) collective-permute-start(bf16[2,2,48,1536]{3,2,0,1:T(8,128)(2,1)S(1)} %dynamic-slice_bitcast_fusion.4), channel_id=1, source_target_pairs={{0,2},{2,0},{4,6},{6,4},{8,10},{10,8},{12,14},{14,12},{16,18},{18,... | collective-permute-start | bytes 1769480 | tf_op jit(solution)/shard_map/ppermute | solution.py:314
  707.8 23.6 %collective-permute-start.42 = (bf16[2,2,192,384]{3,2,1,0:T(8,128)(2,1)S(1)}, bf16[2,2,192,384]{3,2,1,0:T(8,128)(2,1)S(1)}, u32[]{:S(2)}, u32[]{:S(2)}) collective-permute-start(bf16[2,2,192,384]{3,2,1,0:T(8,128)(2,1)S(1)} %dynamic-slice_bitcast_fusion.3), channel_id=1, source_target_pairs={{0,2},{2,0},{4,6},{6,4},{8,10},{10,8},{12,14},{14,12},{16,18},{18,... | collective-permute-start | bytes 1769480 | tf_op jit(solution)/shard_map/ppermute | solution.py:314
  708.6 24.9 %collective-permute-start.47 = (bf16[2,2,192,384]{3,2,0,1:T(8,128)(2,1)S(1)}, bf16[2,2,192,384]{3,2,0,1:T(8,128)(2,1)S(1)}, u32[]{:S(2)}, u32[]{:S(2)}) collective-permute-start(bf16[2,2,192,384]{3,2,0,1:T(8,128)(2,1)S(1)} %dynamic-slice_bitcast_fusion.2), channel_id=1, source_target_pairs={{0,4},{2,6},{4,0},{6,2},{8,12},{10,14},{12,8},{14,10},{16,20},{18,... | collective-permute-start | bytes 1769480 | tf_op jit(solution)/shard_map/ppermute | solution.py:314
  729.3 12.7 %collective-permute-start.33 = (bf16[2,48,1536]{2,1,0:T(8,128)(2,1)S(1)}, bf16[2,48,1536]{2,1,0:T(8,128)(2,1)S(1)}, u32[]{:S(2)}, u32[]{:S(2)}) collective-permute-start(bf16[2,48,1536]{2,1,0:T(8,128)(2,1)S(1)} %dynamic-slice_bitcast_fusion.11), channel_id=1, source_target_pairs={{0,2},{2,0},{4,6},{6,4},{8,10},{10,8},{12,14},{14,12},{16,18},{18,... | collective-permute-start | bytes 884744 | tf_op jit(solution)/shard_map/ppermute | solution.py:314
  731.2 12.4 %collective-permute-start.38 = (bf16[2,48,1536]{2,1,0:T(8,128)(2,1)S(1)}, bf16[2,48,1536]{2,1,0:T(8,128)(2,1)S(1)}, u32[]{:S(2)}, u32[]{:S(2)}) collective-permute-start(bf16[2,48,1536]{2,1,0:T(8,128)(2,1)S(1)} %dynamic-slice_bitcast_fusion.10), channel_id=1, source_target_pairs={{0,4},{2,6},{4,0},{6,2},{8,12},{10,14},{12,8},{14,10},{16,20},{18,... | collective-permute-start | bytes 884744 | tf_op jit(solution)/shard_map/ppermute | solution.py:314
  731.6 15.9 %collective-permute-start.43 = (bf16[2,192,384]{2,1,0:T(8,128)(2,1)S(1)}, bf16[2,192,384]{2,1,0:T(8,128)(2,1)S(1)}, u32[]{:S(2)}, u32[]{:S(2)}) collective-permute-start(bf16[2,192,384]{2,1,0:T(8,128)(2,1)S(1)} %dynamic-slice_bitcast_fusion.9), channel_id=1, source_target_pairs={{0,4},{2,6},{4,0},{6,2},{8,12},{10,14},{12,8},{14,10},{16,20},{18,... | collective-permute-start | bytes 884744 | tf_op jit(solution)/shard_map/ppermute | solution.py:314
  733.8 14.2 %collective-permute-start.48 = (bf16[2,192,384]{2,1,0:T(8,128)(2,1)S(1)}, bf16[2,192,384]{2,1,0:T(8,128)(2,1)S(1)}, u32[]{:S(2)}, u32[]{:S(2)}) collective-permute-start(bf16[2,192,384]{2,1,0:T(8,128)(2,1)S(1)} %dynamic-slice_bitcast_fusion.8), channel_id=1, source_target_pairs={{0,8},{2,10},{4,12},{6,14},{8,0},{10,2},{12,4},{14,6},{16,24},{18,... | collective-permute-start | bytes 884744 | tf_op jit(solution)/shard_map/ppermute | solution.py:314
  743.7 8.2 %collective-permute-start.39 = (bf16[48,1536]{1,0:T(8,128)(2,1)S(1)}, bf16[48,1536]{1,0:T(8,128)(2,1)S(1)}, u32[]{:S(2)}, u32[]{:S(2)}) collective-permute-start(bf16[48,1536]{1,0:T(8,128)(2,1)S(1)} %dynamic-slice_bitcast_fusion.16), channel_id=1, source_target_pairs={{0,8},{2,10},{4,12},{6,14},{8,0},{10,2},{12,4},{14,6},{16,24},{18,... | collective-permute-start | bytes 442376 | tf_op jit(solution)/shard_map/ppermute | solution.py:314
  (200 other events, 1828.8 us)
